TPU v7x, 32 devices: a whole 2x2x4 slice. The times are simulated.
32 devices in a mesh: row: 4 (over x, core), col: 8 (over z, y).
Axes of the slice: x: 2, y: 2, z: 4, core: 2. Of those that a mesh axis runs over, the one named last changes fastest.
Arguments:
- inputs: bfloat16 [64, 128, 256], P('row', 'col'), may hold values from -6 to 6
- stored: bfloat16 [64, 128, 256], P('row', 'col'), may hold values from -6 to 6
- upstream: bfloat16 [64, 128, 256], P('row', 'col'), may hold values from -6 to 6
- weight_in: bfloat16 [256, 1024], replicated, may hold values from -0.375 to 0.375
- weight_out: bfloat16 [1024, 256], replicated, may hold values from -0.1875 to 0.1875
- kernel: bfloat16 [27, 27, 256], replicated, may hold values from -0.21875 to 0.21875
Outputs:
- grad_inputs: bfloat16 [64, 128, 256], P('row', 'col')
- grad_weight_in: bfloat16 [256, 1024], replicated
- grad_weight_out: bfloat16 [1024, 256], replicated
- grad_kernel: bfloat16 [27, 27, 256], replicated
All inputs are finite; a program needn't handle non-finite values.
Results may differ from a plain program's by a relative error of at most 0.0052.
Values may be sent and summed in bfloat16 or wider, within the bound.
A program may use at most 64 MiB of HBM per device.

v0:
```python
import math

import jax
import jax.numpy as jnp
from jax import lax
from jax.sharding import PartitionSpec as P

KS = 27


gelu_coef = 0.044715
root_coef = math.sqrt(2.0 / math.pi)


def padded_2(block, sides, width):
    for axis, dim in sides:
        count = lax.axis_size(axis)
        forward = [(i, i + 1) for i in range(count - 1)]
        backward = [(target, source) for source, target in forward]
        low = lax.ppermute(
            lax.slice_in_dim(block, block.shape[dim] - width, None, axis=dim), axis, forward
        )
        high = lax.ppermute(lax.slice_in_dim(block, 0, width, axis=dim), axis, backward)
        block = jnp.concatenate([low, block, high], axis=dim)
    return block


def gelu_parts(values):
    tanh_part = jnp.tanh(root_coef * (values + gelu_coef * values * values * values))
    result = 0.5 * values * (1.0 + tanh_part)
    slopes = 0.5 * (1.0 + tanh_part) + 0.5 * values * (1.0 - tanh_part * tanh_part) * root_coef * (
        1.0 + 3.0 * gelu_coef * values * values
    )
    return (result, slopes)


def per_device(inputs, stored, upstream, weight_in, weight_out, kernel):
    tile_rows, tile_cols, channels = stored.shape
    radius = KS // 2
    flat_z = stored.reshape(tile_rows * tile_cols, channels)
    flat_g = upstream.reshape(tile_rows * tile_cols, channels)
    hidden = jnp.dot(flat_z, weight_in, preferred_element_type=jnp.float32)
    values, slopes = gelu_parts(hidden)
    active = values.astype(jnp.bfloat16)
    back_proj = jnp.einsum("nc,fc->nf", flat_g, weight_out, preferred_element_type=jnp.float32)
    grad_hidden = (back_proj * slopes).astype(jnp.bfloat16)
    grad_flat = (
        flat_g.astype(jnp.float32)
        + jnp.einsum("nf,cf->nc", grad_hidden, weight_in, preferred_element_type=jnp.float32)
    ).astype(jnp.bfloat16)
    sum_in = jnp.einsum("nc,nf->cf", flat_z, grad_hidden, preferred_element_type=jnp.float32)
    sum_out = jnp.einsum("nf,nc->fc", active, flat_g, preferred_element_type=jnp.float32)
    grad_mid = grad_flat.reshape(tile_rows, tile_cols, channels)
    padded = padded_2(grad_mid, (("row", 0), ("col", 1)), radius)
    kernel_wide = kernel.astype(jnp.float32)

    def sweep(row_off, state_pair):
        accumulated, kernel_sums = state_pair
        slab_rows = lax.dynamic_slice_in_dim(padded, 2 * radius - row_off, tile_rows, 0)
        tap_row = lax.dynamic_index_in_dim(kernel_wide, row_off, 0, keepdims=False)
        tap_sums = []
        for offset in range(KS):
            shifted = slab_rows[:, 2 * radius - offset : 2 * radius - offset + tile_cols].astype(
                jnp.float32
            )
            accumulated = accumulated + tap_row[offset] * shifted
            tap_sums.append(jnp.sum(inputs.astype(jnp.float32) * shifted, axis=(0, 1)))
        kernel_sums = lax.dynamic_update_index_in_dim(kernel_sums, jnp.stack(tap_sums), row_off, 0)
        return (accumulated, kernel_sums)

    start = (
        jnp.zeros((tile_rows, tile_cols, channels), jnp.float32),
        jnp.zeros((KS, KS, channels), jnp.float32),
    )
    accumulated, kernel_sums = lax.fori_loop(0, KS, sweep, start)
    grad_inputs = (grad_mid.astype(jnp.float32) + accumulated).astype(jnp.bfloat16)
    devices_all = lax.axis_size("row") * lax.axis_size("col")
    pixel_count = tile_rows * tile_cols * devices_all
    grad_scale = 1.0 / math.sqrt(pixel_count)
    total_in, total_out, total_kernel = lax.psum((sum_in, sum_out, kernel_sums), ("row", "col"))
    final_in = (total_in * grad_scale).astype(jnp.bfloat16)
    final_out = (total_out * grad_scale).astype(jnp.bfloat16)
    final_kernel = (total_kernel * grad_scale).astype(jnp.bfloat16)
    return (grad_inputs, final_in, final_out, final_kernel)


def solution(mesh):
    return jax.shard_map(
        per_device,
        mesh=mesh,
        in_specs=(
            P("row", "col", None),
            P("row", "col", None),
            P("row", "col", None),
            P(),
            P(),
            P(),
        ),
        out_specs=(P("row", "col", None), P(), P(), P()),
        check_vma=False,
    )
```

profile of v0, /device:TPU:1, one launch (start us, length us, event | category | flops | bytes accessed | tf_op | source)
XLA Modules:
  0.0 314.7 jit_solution(11850986738625315115)
XLA Ops:
  10.8 2.1 collective-permute-start.1
  12.9 4.5 %collective-permute-start = (bf16[13,16,256]{2,1,0:T(8,128)(2,1)S(1)}, bf16[13,16,256]{2,1,0:T(8,128)(2,1)S(1)}, u32[]{:S(2)}, u32[]{:S(2)}) collective-permute-start(bf16[13,16,256]{2,1,0:T(8,128)(2,1)S(1)} %bitcast.190), channel_id=1, source_target_pairs={{0,8},{8,16},{16,24},{1,9},{9,17},{17,25},{2,10},{10,18},{18,26},{... | collective-permute-start | bytes 319496 | tf_op jit(solution)/shard_map/ppermute | solution.py:20
  19.3 3.2 %collective-permute-start.2 = (bf16[42,13,256]{2,1,0:T(8,128)(2,1)S(1)}, bf16[42,13,256]{2,1,0:T(8,128)(2,1)S(1)}, u32[]{:S(2)}, u32[]{:S(2)}) collective-permute-start(bf16[42,13,256]{2,1,0:T(8,128)(2,1)S(1)} %get-tuple-element.255), channel_id=1, source_target_pairs={{0,1},{1,2},{2,3},{3,4},{4,5},{5,6},{6,7},{8,9},{9,10},{10,11},{11... | collective-permute-start | bytes 838664 | tf_op jit(solution)/shard_map/ppermute | solution.py:20
  25.4 12.1 %collective-permute-done.2 = bf16[42,13,256]{2,1,0:T(8,128)(2,1)S(1)} collective-permute-done((bf16[42,13,256]{2,1,0:T(8,128)(2,1)S(1)}, bf16[42,13,256]{2,1,0:T(8,128)(2,1)S(1)}, u32[]{:S(2)}, u32[]{:S(2)}) %collective-permute-start.2) | collective-permute-done | bytes 279584 | tf_op jit(solution)/shard_map/ppermute | solution.py:20
  37.9 126.3 %while.18 = (s32[]{:T(128)}, f32[16,16,256]{2,1,0:T(8,128)S(1)}, f32[27,27,256]{2,1,0:T(8,128)}, f32[27,27,256]{2,1,0:T(8,128)S(1)}, bf16[42,42,256]{2,1,0:T(8,1...) while((s32[]{:T(128)}, f32[16,16,256]{2,1,0:T(8,128)S(1)}, ...), condition=%wide.region_28.29_spmd.clone, body=%wide.region_0.28_spmd.clone.sunk | while | flops 10806561 | bytes 8091645 | solution.py:75
  40.0 2.1 fusion.85
  44.7 2.1 fusion.85
  49.3 2.1 fusion.85
  54.0 2.1 fusion.85
  58.7 2.1 fusion.85
  63.3 2.1 fusion.85
  68.0 2.1 fusion.85
  72.7 2.1 fusion.85
  77.3 2.1 fusion.85
  82.0 2.1 fusion.85
  86.7 2.1 fusion.85
  91.4 2.1 fusion.85
  96.0 2.1 fusion.85
  100.7 2.1 fusion.85
  105.4 2.1 fusion.85
  110.1 2.1 fusion.85
  114.7 2.1 fusion.85
  119.4 2.1 fusion.85
  124.1 2.1 fusion.85
  128.8 2.1 fusion.85
  133.5 2.1 fusion.85
  138.1 2.1 fusion.85
  142.8 2.1 fusion.85
  147.5 2.1 fusion.85
  152.2 2.1 fusion.85
  156.8 2.1 fusion.85
  164.9 137.7 %all-reduce.3.cloned.1.call-done = (f32[256,1024]{0,1:T(8,128)}, f32[1024,256]{1,0:T(8,128)}, f32[27,27,256]{2,1,0:T(8,128)}) async-done(((f32[256,1024]{0,1:T(8,128)}, f32[1024,256]{1,0:T(8,128)}, f32[27,27,256]{2,1,0:T(8,128)}), (f32[256,1024]{0,1:T(8,128)}, f32[1024,256]{1,0:T(8,128)}, f32[27,27,256]{2,1,0:T(8,128)})) %all-reduce.3.cloned.1.call-update) | async-done | bytes 2843664 | tf_op jit(solution)/shard_map/psum | solution.py:80
  (204 shorter events, 87.2 us)
Async XLA Ops:
  7.2 1.0 copy-start
  7.2 2.3 copy-start.8
  7.2 2.3 copy-start.7
  7.2 295.4 %all-reduce.3.cloned.1.call-start = ((), (), s32[]{:S(2)}) async-start(), calls=%async_computation | async-start | bytes 5963776 | tf_op jit(solution)/shard_map/psum | solution.py:80
  9.4 1.0 copy-start.3
  10.5 7.0 %copy-start.5 = (bf16[16,16,256]{2,1,0:T(8,128)(2,1)S(1)}, bf16[16,16,256]{2,1,0:T(8,128)(2,1)}, u32[]{:S(2)}) copy-start(bf16[16,16,256]{2,1,0:T(8,128)(2,1)} %param.9) | copy-start | bytes 393220
  10.8 8.0 %copy-start.6 = (bf16[27,27,256]{2,1,0:T(8,128)(2,1)S(1)}, bf16[27,27,256]{2,1,0:T(8,128)(2,1)}, u32[]{:S(2)}) copy-start(bf16[27,27,256]{2,1,0:T(8,128)(2,1)} %param.13) | copy-start | bytes 1119748
  10.8 8.0 %collective-permute-start.1 = (bf16[13,16,256]{2,1,0:T(8,128)(2,1)S(1)}, bf16[13,16,256]{2,1,0:T(8,128)(2,1)S(1)}, u32[]{:S(2)}, u32[]{:S(2)}) collective-permute-start(bf16[13,16,256]{2,1,0:T(8,128)(2,1)S(1)} %bitcast.191), channel_id=1, source_target_pairs={{8,0},{16,8},{24,16},{9,1},{17,9},{25,17},{10,2},{18,10},{26,18},{... | collective-permute-start | bytes 319496 | tf_op jit(solution)/shard_map/ppermute | solution.py:23
  12.9 6.2 %collective-permute-start = (bf16[13,16,256]{2,1,0:T(8,128)(2,1)S(1)}, bf16[13,16,256]{2,1,0:T(8,128)(2,1)S(1)}, u32[]{:S(2)}, u32[]{:S(2)}) collective-permute-start(bf16[13,16,256]{2,1,0:T(8,128)(2,1)S(1)} %bitcast.190), channel_id=1, source_target_pairs={{0,8},{8,16},{16,24},{1,9},{9,17},{17,25},{2,10},{10,18},{18,26},{... | collective-permute-start | bytes 319496 | tf_op jit(solution)/shard_map/ppermute | solution.py:20
  18.9 4.9 %copy-start.4 = (f32[256,1024]{1,0:T(8,128)S(1)}, f32[256,1024]{1,0:T(8,128)}, u32[]{:S(2)}) copy-start(f32[256,1024]{1,0:T(8,128)} %copy-done.3) | copy-start | bytes 3145732
  19.3 18.2 %collective-permute-start.2 = (bf16[42,13,256]{2,1,0:T(8,128)(2,1)S(1)}, bf16[42,13,256]{2,1,0:T(8,128)(2,1)S(1)}, u32[]{:S(2)}, u32[]{:S(2)}) collective-permute-start(bf16[42,13,256]{2,1,0:T(8,128)(2,1)S(1)} %get-tuple-element.255), channel_id=1, source_target_pairs={{0,1},{1,2},{2,3},{3,4},{4,5},{5,6},{6,7},{8,9},{9,10},{10,11},{11... | collective-permute-start | bytes 838664 | tf_op jit(solution)/shard_map/ppermute | solution.py:20
  22.5 15.0 %collective-permute-start.3 = (bf16[42,13,256]{2,1,0:T(8,128)(2,1)S(1)}, bf16[42,13,256]{2,1,0:T(8,128)(2,1)S(1)}, u32[]{:S(2)}, u32[]{:S(2)}) collective-permute-start(bf16[42,13,256]{2,1,0:T(8,128)(2,1)S(1)} %get-tuple-element.256), channel_id=1, source_target_pairs={{1,0},{2,1},{3,2},{4,3},{5,4},{6,5},{7,6},{9,8},{10,9},{11,10},{12... | collective-permute-start | bytes 838664 | tf_op jit(solution)/shard_map/ppermute | solution.py:23
  25.4 12.5 %copy-start.1 = (bf16[16,16,256]{2,1,0:T(8,128)(2,1)S(1)}, bf16[16,16,256]{2,1,0:T(8,128)(2,1)}, u32[]{:S(2)}) copy-start(bf16[16,16,256]{2,1,0:T(8,128)(2,1)} %param.8) | copy-start | bytes 393220
  303.9 3.0 copy-start.2
Sparse Core Ops, SparseCore 0:
  164.3 138.2 all-reduce.2
where the time goes:
time: 317 us; the launch traced here: 315 us
  waiting for transfers between devices  150 us (47%)
  other arithmetic  109 us (34%)
  local copies, waits for them, and re-layouts  25.2 us (8%)
  between operations  14.2 us (4%)
  starting transfers between devices  11.1 us (4%)
  matrix products  5.29 us (2%)
    psum x1, waiting for transfers between devices, per_device(): lax.psum((sum_in, sum_out, kernel_sums), ('row', 'col'))  138 us
    add x27, other arithmetic, sweep(): accumulated = accumulated + tap_row[offset] * shifted  55.4 us
    reduce_sum x54, other arithmetic, sweep(): tap_sums.append(jnp.sum(inputs.astype(jnp.float32) * shifted, axis=(0, 1)))  47.7 us
    dynamic_update_slice x27, local copies, waits for them, and re-layouts, sweep(): lax.dynamic_update_index_in_dim(kernel_sums, jnp.stack(tap_sums), row_off...  16.5 us
    ppermute x2, waiting for transfers between devices, padded_2(): lax.ppermute(lax.slice_in_dim(block, block.shape[dim] - width, None, axis...  12.3 us
    ppermute x2, starting transfers between devices, padded_2(): lax.ppermute(lax.slice_in_dim(block, block.shape[dim] - width, None, axis...  7.63 us
  transfers between devices with their start and end apart: 5, of which 3 were waited for; matrix products, arithmetic and copies ran while one was open for 1% of the time, Pallas kernels for 0%

commit v1 on v0

--- a/solution.py
+++ b/solution.py
@@ -3,6 +3,8 @@
 import jax
 import jax.numpy as jnp
 from jax import lax
+from jax.experimental import pallas as pl
+from jax.experimental.pallas import tpu as pltpu
 from jax.sharding import PartitionSpec as P
 
 KS = 27
@@ -34,7 +36,7 @@
     return (result, slopes)
 
 
-def per_device(inputs, stored, upstream, weight_in, weight_out, kernel):
+def sweep_device(inputs, stored, upstream, weight_in, weight_out, kernel):
     tile_rows, tile_cols, channels = stored.shape
     radius = KS // 2
     flat_z = stored.reshape(tile_rows * tile_cols, channels)
@@ -84,6 +86,363 @@
     return (grad_inputs, final_in, final_out, final_kernel)
 
 
+MESH = pl.DeviceIdType.MESH
+LANE = 128
+SUB = 8
+
+
+def round_up(value, unit):
+    return -(-value // unit) * unit
+
+
+def dot(a, b, over_a, over_b):
+    return lax.dot_general(
+        a, b, (((over_a,), (over_b,)), ((), ())), preferred_element_type=jnp.float32
+    )
+
+
+def roll_left(v, shift, axis):
+    size = v.shape[axis]
+    shift = shift % size
+    return v if shift == 0 else pltpu.roll(v, size - shift, axis)
+
+
+def moved(v, rows, cols, d_row, d_col):
+    tile = lax.broadcasted_iota(jnp.int32, v.shape, 0)
+    row, col = tile // cols + d_row, tile % cols + d_col
+    inside = (row >= 0) & (row < rows) & (col >= 0) & (col < cols)
+    return jnp.where(inside, roll_left(v, d_row * cols + d_col, 0), 0.0)
+
+
+def bytes_of(ref, sem):
+    pltpu.make_async_copy(ref, ref, sem).wait()
+
+
+def fused_kernel(
+    rows, cols, tile_cols, radius, scale,
+    x_ref, z_ref, g_ref, wi_ref, wo_ref, k_ref,
+    gi_ref, gwi_ref, gwo_ref, gk_ref,
+    x_send, x_recv, g_send, g_recv, o_send, o_recv,
+    part, l1, half, l2, allq, gk_send, gk_recv,
+    wide, x3, g3, o3, taps, taps_t, skew, folded, bands, k_mat, m_mat, x_sh, gk_t,
+    ssem, rsem,
+):
+    n = rows * cols
+    pixels, channels = z_ref.shape
+    own = channels // n
+    side = k_ref.shape[0]
+    lead = pixels - tile_cols * radius - tile_cols
+    width = skew.shape[2]
+    span = 3 * pixels
+    per_block = LANE // tile_cols
+    chunks = pixels // tile_cols
+    my_row, my_col = lax.axis_index("row"), lax.axis_index("col")
+    me = my_row * cols + my_col
+    f32, bf16 = jnp.float32, jnp.bfloat16
+
+    def send(src, dst, phase, row, col):
+        pltpu.make_async_remote_copy(
+            src_ref=src, dst_ref=dst, send_sem=ssem.at[phase], recv_sem=rsem.at[phase],
+            device_id=(row, col), device_id_type=MESH,
+        ).start()
+
+    def to_all(fn):
+        @pl.loop(1, n)
+        def _(p):
+            target = lax.rem(me + p, n)
+            fn(target, target // cols, lax.rem(target, cols))
+
+    barrier = pltpu.get_barrier_semaphore()
+    to_all(lambda t, r, c: pl.semaphore_signal(
+        barrier, inc=1, device_id=(r, c), device_id_type=MESH))
+
+    x_send[...] = x_ref[...].astype(f32).T.reshape(n, own, pixels).astype(bf16)
+    x_recv[pl.ds(me, 1)] = x_send[pl.ds(me, 1)]
+    pl.semaphore_wait(barrier, n - 1)
+    to_all(lambda t, r, c: send(x_send.at[t], x_recv.at[me], 0, r, c))
+
+    z, g = z_ref[...], g_ref[...]
+    total = g.astype(f32)
+    block = wi_ref.shape[1] // rows
+    for f in range(rows):
+        w_in = wi_ref[:, f * block:(f + 1) * block]
+        w_out = wo_ref[f * block:(f + 1) * block, :]
+        values, slopes = gelu_parts(dot(z, w_in, 1, 0))
+        active = values.astype(bf16)
+        grad_hidden = (dot(g, w_out, 1, 1) * slopes).astype(bf16)
+        total = total + dot(grad_hidden, w_in, 1, 1)
+        part[f, :channels] = dot(z, grad_hidden, 0, 0).astype(bf16)
+        part[f, channels:] = dot(active, g, 0, 0).astype(bf16)
+    g_send[...] = total.T.reshape(n, own, pixels).astype(bf16)
+    g_recv[pl.ds(me, 1)] = g_send[pl.ds(me, 1)]
+    to_all(lambda t, r, c: send(g_send.at[t], g_recv.at[me], 1, r, c))
+    for p in range(1, rows):
+        r = lax.rem(my_row + p, rows)
+        send(part.at[r], l1.at[my_row], 2, r, my_col)
+    l1[pl.ds(my_row, 1)] = part[pl.ds(my_row, 1)]
+
+    taps[...] = jnp.zeros_like(taps)
+    for a in range(side):
+        tap = k_ref[a].astype(f32)
+        at = lead + tile_cols * a
+        taps[0, at:at + radius + 1, :] = tap[radius:]
+        taps[1, at + tile_cols - radius:at + tile_cols, :] = tap[:radius]
+    lanes_at = pl.multiple_of(me * own // LANE * LANE, LANE)
+    for sign in range(2):
+        taps_t[...] = taps[sign, :, pl.ds(lanes_at, LANE)].T
+        line = taps_t[pl.ds(pl.multiple_of(lax.rem(me * own, LANE), SUB), own), :]
+        for t in range(SUB):
+            skew[sign * own:(sign + 1) * own, t, :] = pltpu.roll(line, t, 1) if t else line
+
+    at_or_after = (
+        lax.broadcasted_iota(jnp.int32, (tile_cols, span), 1) % tile_cols
+        >= lax.broadcasted_iota(jnp.int32, (tile_cols, span), 0)
+    )
+    offsets = (-1, 0, 1)
+
+    bytes_of(x_recv.at[pl.ds(0, n - 1)], rsem.at[0])
+    wide[...] = x_recv[...].astype(f32)
+    for c in range(own):
+        x3[c] = wide[:, c, :]
+    bytes_of(g_recv.at[pl.ds(0, n - 1)], rsem.at[1])
+    wide[...] = g_recv[...].astype(f32)
+    for c in range(own):
+        g3[c] = wide[:, c, :]
+
+    @pl.loop(0, own)
+    def _(c):
+        here = x3[c]
+        for i, d_col in enumerate(offsets):
+            for j, d_row in enumerate(offsets):
+                at = i * span + j * pixels
+                x_sh[:, at:at + pixels] = moved(here, rows, cols, d_row, d_col).astype(bf16)
+        m_mat[...] = dot(g3[c].astype(bf16), x_sh[...], 0, 0)
+
+        def piece(q, i):
+            return m_mat[q * tile_cols:(q + 1) * tile_cols, i * span:(i + 1) * span]
+
+        def lagged(q, sign):
+            after, before = ((1, 2), (0, 1))[sign]
+            out = jnp.zeros((tile_cols, span), f32)
+            if q >= 1:
+                out = jnp.where(at_or_after, piece(q - 1, after), 0.0)
+            if q < chunks:
+                out = out + jnp.where(at_or_after, 0.0, piece(q, before))
+            return out
+
+        for sign in range(2):
+            parts = []
+            for i in range(per_block):
+                v = jnp.zeros((tile_cols, width), f32)
+                for q in range(i, chunks + 1, per_block):
+                    skip = q // per_block * LANE
+                    piece_q = lagged(q, sign)[:, skip:skip + width]
+                    missing = width - piece_q.shape[1]
+                    if missing:
+                        piece_q = jnp.concatenate(
+                            [piece_q, jnp.zeros((tile_cols, missing), f32)], axis=1)
+                    v = v + piece_q
+                parts.append(v)
+            while len(parts) > 1:
+                m = len(parts) // 2
+                parts = [parts[i] + roll_left(parts[i + m], m * tile_cols, 1) for i in range(m)]
+            v = parts[0]
+            m = tile_cols // 2
+            while m >= SUB:
+                v = v[:m] + roll_left(v[m:], m, 1)
+                m //= 2
+            folded[sign * own + c] = v
+
+    lines = folded[:, 0, :]
+    for t in range(1, SUB):
+        lines = lines + roll_left(folded[:, t, :], t, 1)
+    keep = gk_send.shape[1] // 2
+    lines = (lines * scale)[:, :keep]
+    gk_send[...] = jnp.concatenate([lines[:own], lines[own:]], axis=1).astype(bf16)
+    gk_recv[pl.ds(me, 1)] = gk_send[...][None]
+    to_all(lambda t, r, c: send(gk_send, gk_recv.at[me], 6, r, c))
+
+    bytes_of(l1.at[pl.ds(0, rows - 1)], rsem.at[2])
+    for j in range(cols):
+        size = half.shape[1]
+        v = l1[0, j * size:(j + 1) * size, :].astype(f32)
+        for r in range(1, rows):
+            v = v + l1[r, j * size:(j + 1) * size, :].astype(f32)
+        half[j] = v.astype(bf16)
+    for p in range(1, cols):
+        c = lax.rem(my_col + p, cols)
+        send(half.at[c], l2.at[my_col], 3, my_row, c)
+    l2[pl.ds(my_col, 1)] = half[pl.ds(my_col, 1)]
+
+    bands[...] = jnp.zeros_like(bands)
+    @pl.loop(0, own)
+    def _(c):
+        for sign in range(2):
+            v = skew[sign * own + c]
+            m = SUB
+            while m < tile_cols:
+                v = jnp.concatenate([v, pltpu.roll(v, m, 1)], axis=0)
+                m *= 2
+            parts = [v]
+            while len(parts) < per_block:
+                m = len(parts) * tile_cols
+                parts = parts + [pltpu.roll(u, m, 1) for u in parts]
+            for i, u in enumerate(parts):
+                bands[sign, i * tile_cols:(i + 1) * tile_cols, pixels:pixels + width] = u
+
+        def band(q, sign):
+            at = q % per_block * tile_cols
+            skip = pixels - q // per_block * LANE
+            return bands[sign, at:at + tile_cols, skip:skip + span]
+
+        for q in range(chunks):
+            at = slice(q * tile_cols, (q + 1) * tile_cols)
+            k_mat[at, :span] = jnp.where(at_or_after, band(q + 1, 1), 0.0).astype(bf16)
+            k_mat[at, span:2 * span] = jnp.where(
+                at_or_after, band(q + 1, 0), band(q, 1)).astype(bf16)
+            k_mat[at, 2 * span:] = jnp.where(at_or_after, 0.0, band(q, 0)).astype(bf16)
+        here = g3[c]
+        spread = dot(here.astype(bf16), k_mat[...], 1, 0)
+        result = here
+        for i, d_col in enumerate(offsets):
+            for j, d_row in enumerate(offsets):
+                at = i * span + j * pixels
+                result = result + moved(spread[:, at:at + pixels], rows, cols, -d_row, -d_col)
+        o3[c] = result
+
+    for c in range(own):
+        wide[:, c, :] = o3[c]
+    o_send[...] = wide[...].astype(bf16)
+    o_recv[pl.ds(me, 1)] = o_send[pl.ds(me, 1)]
+    to_all(lambda t, r, c: send(o_send.at[t], o_recv.at[me], 7, r, c))
+
+    bytes_of(l2.at[pl.ds(0, cols - 1)], rsem.at[3])
+    v = l2[0].astype(f32)
+    for c in range(1, cols):
+        v = v + l2[c].astype(f32)
+    mine = allq.at[my_row, my_col]
+    mine[...] = (v * scale).astype(bf16)
+    for p in range(1, cols):
+        send(mine, mine, 4, my_row, lax.rem(my_col + p, cols))
+
+    bytes_of(allq.at[0, pl.ds(0, cols - 1)], rsem.at[4])
+    for p in range(1, rows):
+        send(allq.at[my_row], allq.at[my_row], 5, lax.rem(my_row + p, rows), my_col)
+
+    bytes_of(o_recv.at[pl.ds(0, n - 1)], rsem.at[7])
+    gi_ref[...] = o_recv[...].astype(f32).reshape(channels, pixels).T.astype(bf16)
+
+    bytes_of(gk_recv.at[pl.ds(0, n - 1)], rsem.at[6])
+    gk_t[...] = gk_recv[...].astype(f32).reshape(channels, 2 * keep).T
+    for a in range(side):
+        at = lead + tile_cols * a
+        low = gk_t[keep + at + tile_cols - radius:keep + at + tile_cols, :]
+        high = gk_t[at:at + radius + 1, :]
+        gk_ref[a] = jnp.concatenate([low, high], axis=0).astype(bf16)
+
+    bytes_of(allq.at[pl.ds(0, rows - 1)], rsem.at[5])
+    per_half = cols // 2
+    for f in range(rows):
+        at = slice(f * block, (f + 1) * block)
+        gwi_ref[:, at] = allq[f, :per_half].reshape(channels, block)
+        gwo_ref[at, :] = allq[f, per_half:].reshape(block, channels)
+
+    bytes_of(x_send.at[pl.ds(0, n - 1)], ssem.at[0])
+    bytes_of(g_send.at[pl.ds(0, n - 1)], ssem.at[1])
+    bytes_of(part.at[pl.ds(0, rows - 1)], ssem.at[2])
+    bytes_of(half.at[pl.ds(0, cols - 1)], ssem.at[3])
+    bytes_of(l2.at[pl.ds(0, cols - 1)], ssem.at[4])
+    bytes_of(allq.at[pl.ds(0, rows - 1)], ssem.at[5])
+    bytes_of(gk_recv.at[pl.ds(0, n - 1)], ssem.at[6])
+    bytes_of(o_send.at[pl.ds(0, n - 1)], ssem.at[7])
+
+
+def fits(rows, cols, tile_rows, tile_cols, channels, hidden):
+    n = rows * cols
+    pixels = tile_rows * tile_cols
+    radius = KS // 2
+    return (
+        channels % n == 0
+        and channels // n == SUB
+        and channels % LANE == 0
+        and rows > 1
+        and cols % 2 == 0
+        and hidden == rows * channels
+        and pixels == 2 * LANE
+        and tile_cols == 2 * SUB
+        and radius < min(tile_rows, tile_cols)
+        and (2 * channels) % (cols * 2 * SUB) == 0
+    )
+
+
+def fused_device(inputs, stored, upstream, weight_in, weight_out, kernel):
+    rows, cols = lax.axis_size("row"), lax.axis_size("col")
+    tile_rows, tile_cols, channels = stored.shape
+    n, pixels, hidden = rows * cols, tile_rows * tile_cols, weight_in.shape[1]
+    side = kernel.shape[0]
+    radius = side // 2
+    own = channels // n
+    taps = pixels - tile_cols * radius - tile_cols + tile_cols * side
+    width = round_up(taps + LANE - 1, LANE)
+    keep = round_up(taps, LANE)
+    span = 3 * pixels
+    scale = 1.0 / math.sqrt(pixels * n)
+    bf16, f32 = jnp.bfloat16, jnp.float32
+    flat = (pixels, channels)
+    piece = 2 * channels // cols
+    vmem = pl.BlockSpec(memory_space=pltpu.VMEM)
+    results = pl.pallas_call(
+        lambda *refs: fused_kernel(rows, cols, tile_cols, radius, scale, *refs),
+        out_shape=(
+            jax.ShapeDtypeStruct(flat, bf16),
+            jax.ShapeDtypeStruct(weight_in.shape, bf16),
+            jax.ShapeDtypeStruct(weight_out.shape, bf16),
+            jax.ShapeDtypeStruct(kernel.shape, bf16),
+        ),
+        in_specs=[vmem] * 6,
+        out_specs=(vmem,) * 4,
+        scratch_shapes=[pltpu.VMEM((n, own, pixels), bf16)] * 6 + [
+            pltpu.VMEM((rows, 2 * channels, channels), bf16),
+            pltpu.VMEM((rows, 2 * channels, channels), bf16),
+            pltpu.VMEM((cols, piece, channels), bf16),
+            pltpu.VMEM((cols, piece, channels), bf16),
+            pltpu.VMEM((rows, cols, piece, channels), bf16),
+            pltpu.VMEM((own, 2 * keep), bf16),
+            pltpu.VMEM((n, own, 2 * keep), bf16),
+            pltpu.VMEM((n, own, pixels), f32),
+            pltpu.VMEM((own, n, pixels), f32),
+            pltpu.VMEM((own, n, pixels), f32),
+            pltpu.VMEM((own, n, pixels), f32),
+            pltpu.VMEM((2, width, channels), f32),
+            pltpu.VMEM((LANE, width), f32),
+            pltpu.VMEM((2 * own, SUB, width), f32),
+            pltpu.VMEM((2 * own, SUB, width), f32),
+            pltpu.VMEM((2, LANE, pixels + span), f32),
+            pltpu.VMEM((pixels, 3 * span), bf16),
+            pltpu.VMEM((pixels, 3 * span), f32),
+            pltpu.VMEM((n, 3 * span), bf16),
+            pltpu.VMEM((2 * keep, channels), f32),
+            pltpu.SemaphoreType.DMA((8,)),
+            pltpu.SemaphoreType.DMA((8,)),
+        ],
+        compiler_params=pltpu.CompilerParams(
+            collective_id=0, has_side_effects=True, vmem_limit_bytes=48 * 1024 * 1024
+        ),
+    )(
+        inputs.reshape(flat), stored.reshape(flat), upstream.reshape(flat),
+        weight_in, weight_out, kernel,
+    )
+    return (results[0].reshape(stored.shape), *results[1:])
+
+
+def per_device(inputs, stored, upstream, weight_in, weight_out, kernel):
+    args = (inputs, stored, upstream, weight_in, weight_out, kernel)
+    sizes = (lax.axis_size("row"), lax.axis_size("col"))
+    if fits(*sizes, *stored.shape, weight_in.shape[1]):
+        return fused_device(*args)
+    return sweep_device(*args)
+
+
 def solution(mesh):
     return jax.shard_map(
         per_device,

time: 317 us -> 69.1 us (0.22)
  waiting for transfers between devices: 150 us -> 0 us
  other arithmetic: 109 us -> 0 us
  Pallas kernels: 0 us -> 58.5 us
  local copies, waits for them, and re-layouts: 25.2 us -> 8.8 us
  between operations: 14.2 us -> 0.66 us
  starting transfers between devices: 11.1 us -> 0 us
  matrix products: 5.29 us -> 0 us
    psum x1 -> x0, waiting for transfers between devices: 138 us -> none  [per_device(): lax.psum((sum_in, sum_out, kernel_sums), ('row', 'col'))]
    pallas_call x0 -> x1, Pallas kernels: none -> 58.5 us  [fused_device(): pl.pallas_call(lambda *refs: fused_kernel(rows, cols, tile_cols, radius,...]
    add x27 -> x0, other arithmetic: 55.4 us -> none  [sweep(): accumulated = accumulated + tap_row[offset] * shifted]
    reduce_sum x54 -> x0, other arithmetic: 47.7 us -> none  [sweep(): tap_sums.append(jnp.sum(inputs.astype(jnp.float32) * shifted, axis=(0, 1)))]
    dynamic_update_slice x27 -> x0, local copies, waits for them, and re-layouts: 16.5 us -> none  [sweep(): lax.dynamic_update_index_in_dim(kernel_sums, jnp.stack(tap_sums), row_off...]
    ppermute x4 -> x0, waiting for transfers between devices: 12.3 us -> none  [the longest x2 12.3 us: padded_2(): lax.ppermute(lax.slice_in_dim(block, block.shape[dim] - width, None, axis...]
    ppermute x4 -> x0, starting transfers between devices: 11 us -> none  [the longest x2 7.63 us: padded_2(): lax.ppermute(lax.slice_in_dim(block, block.shape[dim] - width, None, axis...]
    unnamed x19 -> x16, local copies, waits for them, and re-layouts: 2.23 us -> 8.8 us
  transfers between devices with their start and end apart: 5 -> 0, of which waited for: 3 -> 0; matrix products, arithmetic and copies ran while one was open for 1% -> 0% of each run, Pallas kernels for 0% -> 0%
where the time goes in v1:
time: 69.1 us; the launch traced here: 67.9 us
  Pallas kernels  58.5 us (85%)
  local copies, waits for them, and re-layouts  8.8 us (13%)
    pallas_call x1, Pallas kernels, fused_device(): pl.pallas_call(lambda *refs: fused_kernel(rows, cols, tile_cols, radius,...  58.5 us
    unnamed x16, local copies, waits for them, and re-layouts  8.8 us

profile of v1, /device:TPU:1, one launch (start us, length us, event | category | flops | bytes accessed | tf_op | source)
XLA Modules:
  0.0 67.9 jit_solution(8141269103796929060)
XLA Ops:
  0.6 0.0 copy-start
  0.6 1.0 %copy-done = bf16[256,1024]{1,0:T(8,128)(2,1)S(1)} copy-done((bf16[256,1024]{1,0:T(8,128)(2,1)S(1)}, bf16[256,1024]{1,0:T(8,128)(2,1)}, u32[]{:S(2)}) %copy-start) | copy-done | bytes 524312
  1.7 0.0 copy-start.1
  1.7 1.0 %copy-done.1 = bf16[1024,256]{1,0:T(8,128)(2,1)S(1)} copy-done((bf16[1024,256]{1,0:T(8,128)(2,1)S(1)}, bf16[1024,256]{1,0:T(8,128)(2,1)}, u32[]{:S(2)}) %copy-start.1) | copy-done | bytes 524312
  2.7 0.0 copy-start.2
  2.7 1.0 %copy-done.2 = bf16[27,27,256]{2,1,0:T(8,128)(2,1)S(1)} copy-done((bf16[27,27,256]{2,1,0:T(8,128)(2,1)S(1)}, bf16[27,27,256]{2,1,0:T(8,128)(2,1)}, u32[]{:S(2)}) %copy-start.2) | copy-done | bytes 373272
  3.7 0.0 copy-start.3
  3.7 0.9 %copy-done.3 = bf16[16,16,256]{2,1,0:T(8,128)(2,1)S(1)} copy-done((bf16[16,16,256]{2,1,0:T(8,128)(2,1)S(1)}, bf16[16,16,256]{2,1,0:T(8,128)(2,1)}, u32[]{:S(2)}) %copy-start.3) | copy-done | bytes 131096
  4.6 0.0 copy-start.4
  4.6 0.9 %copy-done.4 = bf16[16,16,256]{2,1,0:T(8,128)(2,1)S(1)} copy-done((bf16[16,16,256]{2,1,0:T(8,128)(2,1)S(1)}, bf16[16,16,256]{2,1,0:T(8,128)(2,1)}, u32[]{:S(2)}) %copy-start.4) | copy-done | bytes 131096
  5.5 0.0 copy-start.5
  5.5 0.9 %copy-done.5 = bf16[16,16,256]{2,1,0:T(8,128)(2,1)S(1)} copy-done((bf16[16,16,256]{2,1,0:T(8,128)(2,1)S(1)}, bf16[16,16,256]{2,1,0:T(8,128)(2,1)}, u32[]{:S(2)}) %copy-start.5) | copy-done | bytes 131096
  6.4 58.5 %shard_map.93 = (bf16[256,256]{1,0:T(8,128)(2,1)S(1)}, bf16[256,1024]{1,0:T(8,128)(2,1)S(1)}, bf16[1024,256]{1,0:T(8,128)(2,1)S(1)}, bf16[27,27,256]{2,1,0:T(8,128)(2,1)S(1)}) custom-call(bf16[256,256]{1,0:T(8,128)(2,1)S(1)} %bitcast.4, bf16[256,256]{1,0:T(8,128)(2,1)S(1)} %bitcast.5, bf16[256,256]{1,0:T(8,128)(2,1)S(1)} %bitcast.6, ...), custom_call_target="tpu_custom_call" | custom-call | tf_op jit(solution)/shard_map/pallas_call | solution.py:394
  64.9 0.7 copy.14
  65.6 0.8 %copy.15 = bf16[256,1024]{1,0:T(8,128)(2,1)} copy(bf16[256,1024]{1,0:T(8,128)(2,1)S(1)} %get-tuple-element.17) | data formatting | bytes 1048576
  66.4 0.8 %copy.16 = bf16[1024,256]{1,0:T(8,128)(2,1)} copy(bf16[1024,256]{1,0:T(8,128)(2,1)S(1)} %get-tuple-element.18) | data formatting | bytes 1048576
  67.2 0.8 %copy.17 = bf16[27,27,256]{2,1,0:T(8,128)(2,1)} copy(bf16[27,27,256]{2,1,0:T(8,128)(2,1)S(1)} %get-tuple-element.19) | data formatting | bytes 746496
Async XLA Ops:
  0.6 1.0 %copy-start = (bf16[256,1024]{1,0:T(8,128)(2,1)S(1)}, bf16[256,1024]{1,0:T(8,128)(2,1)}, u32[]{:S(2)}) copy-start(bf16[256,1024]{1,0:T(8,128)(2,1)} %refs_3_.1) | copy-start | bytes 1572868
  1.7 1.0 %copy-start.1 = (bf16[1024,256]{1,0:T(8,128)(2,1)S(1)}, bf16[1024,256]{1,0:T(8,128)(2,1)}, u32[]{:S(2)}) copy-start(bf16[1024,256]{1,0:T(8,128)(2,1)} %refs_4_.1) | copy-start | bytes 1572868
  2.7 1.0 %copy-start.2 = (bf16[27,27,256]{2,1,0:T(8,128)(2,1)S(1)}, bf16[27,27,256]{2,1,0:T(8,128)(2,1)}, u32[]{:S(2)}) copy-start(bf16[27,27,256]{2,1,0:T(8,128)(2,1)} %refs_5_.1) | copy-start | bytes 1119748
  3.7 0.9 %copy-start.3 = (bf16[16,16,256]{2,1,0:T(8,128)(2,1)S(1)}, bf16[16,16,256]{2,1,0:T(8,128)(2,1)}, u32[]{:S(2)}) copy-start(bf16[16,16,256]{2,1,0:T(8,128)(2,1)} %param.6) | copy-start | bytes 393220
  4.6 0.9 %copy-start.4 = (bf16[16,16,256]{2,1,0:T(8,128)(2,1)S(1)}, bf16[16,16,256]{2,1,0:T(8,128)(2,1)}, u32[]{:S(2)}) copy-start(bf16[16,16,256]{2,1,0:T(8,128)(2,1)} %param.7) | copy-start | bytes 393220
  5.5 0.9 %copy-start.5 = (bf16[16,16,256]{2,1,0:T(8,128)(2,1)S(1)}, bf16[16,16,256]{2,1,0:T(8,128)(2,1)}, u32[]{:S(2)}) copy-start(bf16[16,16,256]{2,1,0:T(8,128)(2,1)} %param.8) | copy-start | bytes 393220

commit v2 on v1

--- a/solution.py
+++ b/solution.py
@@ -120,12 +120,13 @@
 
 def fused_kernel(
     rows, cols, tile_cols, radius, scale,
+    x_hbm, z_hbm, g_hbm, wi_hbm, wo_hbm, k_hbm,
+    gi_ref, gwi_ref, gwo_ref, gk_ref,
     x_ref, z_ref, g_ref, wi_ref, wo_ref, k_ref,
-    gi_ref, gwi_ref, gwo_ref, gk_ref,
     x_send, x_recv, g_send, g_recv, o_send, o_recv,
-    part, l1, half, l2, allq, gk_send, gk_recv,
+    part, from_pair, paired, from_rows, half, from_cols, allq, gk_send, gk_recv,
     wide, x3, g3, o3, taps, taps_t, skew, folded, bands, k_mat, m_mat, x_sh, gk_t,
-    ssem, rsem,
+    isem, ssem, rsem,
 ):
     n = rows * cols
     pixels, channels = z_ref.shape
@@ -138,6 +139,9 @@
     chunks = pixels // tile_cols
     my_row, my_col = lax.axis_index("row"), lax.axis_index("col")
     me = my_row * cols + my_col
+    pairs = rows // 2
+    my_pair, core = my_row // 2, lax.rem(my_row, 2)
+    other = 1 - core
     f32, bf16 = jnp.float32, jnp.bfloat16
 
     def send(src, dst, phase, row, col):
@@ -146,21 +150,76 @@
             device_id=(row, col), device_id_type=MESH,
         ).start()
 
+    def sum_pair(s):
+        bytes_of(from_pair.at[s], rsem.at[4 + s])
+        for p in range(pairs):
+            paired[s, p] = (
+                part[s, core, p].astype(f32) + from_pair[s, p].astype(f32)).astype(bf16)
+        for p in range(1, pairs):
+            to = lax.rem(my_pair + p, pairs)
+            send(paired.at[s, to], from_rows.at[s, my_pair], 6 + s, 2 * to + core, my_col)
+        from_rows[s, pl.ds(my_pair, 1)] = paired[s, pl.ds(my_pair, 1)]
+
+    def sum_rows(s):
+        bytes_of(from_rows.at[s, pl.ds(0, pairs - 1)], rsem.at[6 + s])
+        v = from_rows[s, 0].astype(f32)
+        for p in range(1, pairs):
+            v = v + from_rows[s, p].astype(f32)
+        half[s] = v.reshape(half.shape[1:]).astype(bf16)
+        for p in range(1, cols):
+            c = lax.rem(my_col + p, cols)
+            send(half.at[s, c], from_cols.at[s, my_col], 8 + s, my_row, c)
+        from_cols[s, pl.ds(my_col, 1)] = half[s, pl.ds(my_col, 1)]
+
+    def sum_cols(s):
+        bytes_of(from_cols.at[s, pl.ds(0, cols - 1)], rsem.at[8 + s])
+        v = from_cols[s, 0].astype(f32)
+        for c in range(1, cols):
+            v = v + from_cols[s, c].astype(f32)
+        mine = allq.at[s, core, my_pair, my_col]
+        mine[...] = (v * scale).astype(bf16)
+        for p in range(1, cols):
+            send(mine, mine, 10 + s, my_row, lax.rem(my_col + p, cols))
+
+    def share_rows(s):
+        bytes_of(allq.at[s, 0, 0, pl.ds(0, cols - 1)], rsem.at[10 + s])
+        mine = allq.at[s, core, my_pair]
+        for p in range(1, pairs):
+            to = lax.rem(my_pair + p, pairs)
+            send(mine, mine, 12 + s, 2 * to + core, my_col)
+
+    def share_pair(s):
+        bytes_of(allq.at[s, 0, pl.ds(0, pairs - 1)], rsem.at[12 + s])
+        mine = allq.at[s, core]
+        send(mine, mine, 14 + s, my_row + other - core, my_col)
+
     def to_all(fn):
         @pl.loop(1, n)
         def _(p):
             target = lax.rem(me + p, n)
             fn(target, target // cols, lax.rem(target, cols))
 
+    loads = [
+        pltpu.make_async_copy(source, target, isem.at[i])
+        for i, (source, target) in enumerate((
+            (x_hbm, x_ref), (z_hbm, z_ref), (g_hbm, g_ref),
+            (wi_hbm, wi_ref), (wo_hbm, wo_ref), (k_hbm, k_ref),
+        ))
+    ]
+    for load in loads:
+        load.start()
     barrier = pltpu.get_barrier_semaphore()
     to_all(lambda t, r, c: pl.semaphore_signal(
         barrier, inc=1, device_id=(r, c), device_id_type=MESH))
 
+    loads[0].wait()
     x_send[...] = x_ref[...].astype(f32).T.reshape(n, own, pixels).astype(bf16)
     x_recv[pl.ds(me, 1)] = x_send[pl.ds(me, 1)]
     pl.semaphore_wait(barrier, n - 1)
     to_all(lambda t, r, c: send(x_send.at[t], x_recv.at[me], 0, r, c))
 
+    for load in loads[1:]:
+        load.wait()
     z, g = z_ref[...], g_ref[...]
     total = g.astype(f32)
     block = wi_ref.shape[1] // rows
@@ -171,15 +230,13 @@
         active = values.astype(bf16)
         grad_hidden = (dot(g, w_out, 1, 1) * slopes).astype(bf16)
         total = total + dot(grad_hidden, w_in, 1, 1)
-        part[f, :channels] = dot(z, grad_hidden, 0, 0).astype(bf16)
-        part[f, channels:] = dot(active, g, 0, 0).astype(bf16)
+        part[0, f % 2, f // 2] = dot(z, grad_hidden, 0, 0).astype(bf16)
+        part[1, f % 2, f // 2] = dot(active, g, 0, 0).astype(bf16)
     g_send[...] = total.T.reshape(n, own, pixels).astype(bf16)
     g_recv[pl.ds(me, 1)] = g_send[pl.ds(me, 1)]
     to_all(lambda t, r, c: send(g_send.at[t], g_recv.at[me], 1, r, c))
-    for p in range(1, rows):
-        r = lax.rem(my_row + p, rows)
-        send(part.at[r], l1.at[my_row], 2, r, my_col)
-    l1[pl.ds(my_row, 1)] = part[pl.ds(my_row, 1)]
+    for s in range(2):
+        send(part.at[s, other], from_pair.at[s], 4 + s, my_row + other - core, my_col)
 
     taps[...] = jnp.zeros_like(taps)
     for a in range(side):
@@ -200,6 +257,8 @@
     )
     offsets = (-1, 0, 1)
 
+    sum_pair(0)
+    sum_pair(1)
     bytes_of(x_recv.at[pl.ds(0, n - 1)], rsem.at[0])
     wide[...] = x_recv[...].astype(f32)
     for c in range(own):
@@ -209,8 +268,7 @@
     for c in range(own):
         g3[c] = wide[:, c, :]
 
-    @pl.loop(0, own)
-    def _(c):
+    def correlate(c):
         here = x3[c]
         for i, d_col in enumerate(offsets):
             for j, d_row in enumerate(offsets):
@@ -253,6 +311,11 @@
                 m //= 2
             folded[sign * own + c] = v
 
+    pl.loop(0, own // 2)(correlate)
+    sum_rows(0)
+    sum_rows(1)
+    pl.loop(own // 2, own)(correlate)
+
     lines = folded[:, 0, :]
     for t in range(1, SUB):
         lines = lines + roll_left(folded[:, t, :], t, 1)
@@ -260,23 +323,14 @@
     lines = (lines * scale)[:, :keep]
     gk_send[...] = jnp.concatenate([lines[:own], lines[own:]], axis=1).astype(bf16)
     gk_recv[pl.ds(me, 1)] = gk_send[...][None]
-    to_all(lambda t, r, c: send(gk_send, gk_recv.at[me], 6, r, c))
-
-    bytes_of(l1.at[pl.ds(0, rows - 1)], rsem.at[2])
-    for j in range(cols):
-        size = half.shape[1]
-        v = l1[0, j * size:(j + 1) * size, :].astype(f32)
-        for r in range(1, rows):
-            v = v + l1[r, j * size:(j + 1) * size, :].astype(f32)
-        half[j] = v.astype(bf16)
-    for p in range(1, cols):
-        c = lax.rem(my_col + p, cols)
-        send(half.at[c], l2.at[my_col], 3, my_row, c)
-    l2[pl.ds(my_col, 1)] = half[pl.ds(my_col, 1)]
+    to_all(lambda t, r, c: send(gk_send, gk_recv.at[me], 2, r, c))
+
+    sum_cols(0)
+    sum_cols(1)
 
     bands[...] = jnp.zeros_like(bands)
-    @pl.loop(0, own)
-    def _(c):
+
+    def convolve(c):
         for sign in range(2):
             v = skew[sign * own + c]
             m = SUB
@@ -310,29 +364,24 @@
                 result = result + moved(spread[:, at:at + pixels], rows, cols, -d_row, -d_col)
         o3[c] = result
 
+    pl.loop(0, own // 2)(convolve)
+    share_rows(0)
+    share_rows(1)
+    pl.loop(own // 2, own)(convolve)
+
     for c in range(own):
         wide[:, c, :] = o3[c]
     o_send[...] = wide[...].astype(bf16)
     o_recv[pl.ds(me, 1)] = o_send[pl.ds(me, 1)]
-    to_all(lambda t, r, c: send(o_send.at[t], o_recv.at[me], 7, r, c))
-
-    bytes_of(l2.at[pl.ds(0, cols - 1)], rsem.at[3])
-    v = l2[0].astype(f32)
-    for c in range(1, cols):
-        v = v + l2[c].astype(f32)
-    mine = allq.at[my_row, my_col]
-    mine[...] = (v * scale).astype(bf16)
-    for p in range(1, cols):
-        send(mine, mine, 4, my_row, lax.rem(my_col + p, cols))
-
-    bytes_of(allq.at[0, pl.ds(0, cols - 1)], rsem.at[4])
-    for p in range(1, rows):
-        send(allq.at[my_row], allq.at[my_row], 5, lax.rem(my_row + p, rows), my_col)
-
-    bytes_of(o_recv.at[pl.ds(0, n - 1)], rsem.at[7])
+    to_all(lambda t, r, c: send(o_send.at[t], o_recv.at[me], 3, r, c))
+
+    share_pair(0)
+    share_pair(1)
+
+    bytes_of(o_recv.at[pl.ds(0, n - 1)], rsem.at[3])
     gi_ref[...] = o_recv[...].astype(f32).reshape(channels, pixels).T.astype(bf16)
 
-    bytes_of(gk_recv.at[pl.ds(0, n - 1)], rsem.at[6])
+    bytes_of(gk_recv.at[pl.ds(0, n - 1)], rsem.at[2])
     gk_t[...] = gk_recv[...].astype(f32).reshape(channels, 2 * keep).T
     for a in range(side):
         at = lead + tile_cols * a
@@ -340,21 +389,36 @@
         high = gk_t[at:at + radius + 1, :]
         gk_ref[a] = jnp.concatenate([low, high], axis=0).astype(bf16)
 
-    bytes_of(allq.at[pl.ds(0, rows - 1)], rsem.at[5])
-    per_half = cols // 2
+    for s in range(2):
+        bytes_of(allq.at[s, 0], rsem.at[14 + s])
     for f in range(rows):
         at = slice(f * block, (f + 1) * block)
-        gwi_ref[:, at] = allq[f, :per_half].reshape(channels, block)
-        gwo_ref[at, :] = allq[f, per_half:].reshape(block, channels)
+        gwi_ref[:, at] = allq[0, f % 2, f // 2].reshape(channels, block)
+        gwo_ref[at, :] = allq[1, f % 2, f // 2].reshape(block, channels)
 
     bytes_of(x_send.at[pl.ds(0, n - 1)], ssem.at[0])
     bytes_of(g_send.at[pl.ds(0, n - 1)], ssem.at[1])
-    bytes_of(part.at[pl.ds(0, rows - 1)], ssem.at[2])
-    bytes_of(half.at[pl.ds(0, cols - 1)], ssem.at[3])
-    bytes_of(l2.at[pl.ds(0, cols - 1)], ssem.at[4])
-    bytes_of(allq.at[pl.ds(0, rows - 1)], ssem.at[5])
-    bytes_of(gk_recv.at[pl.ds(0, n - 1)], ssem.at[6])
-    bytes_of(o_send.at[pl.ds(0, n - 1)], ssem.at[7])
+    bytes_of(gk_recv.at[pl.ds(0, n - 1)], ssem.at[2])
+    bytes_of(o_send.at[pl.ds(0, n - 1)], ssem.at[3])
+    for s in range(2):
+        bytes_of(from_pair.at[s], ssem.at[4 + s])
+        bytes_of(paired.at[s, pl.ds(0, pairs - 1)], ssem.at[6 + s])
+        bytes_of(half.at[s, pl.ds(0, cols - 1)], ssem.at[8 + s])
+        bytes_of(from_cols.at[s, pl.ds(0, cols - 1)], ssem.at[10 + s])
+        bytes_of(allq.at[s, 0, pl.ds(0, pairs - 1)], ssem.at[12 + s])
+        bytes_of(allq.at[s, 0], ssem.at[14 + s])
+
+
+def hand_over_kernel(*refs):
+    count = len(refs) // 2
+    sem = refs[-1]
+    copies = [
+        pltpu.make_async_copy(refs[i], refs[count + i], sem.at[i]) for i in range(count)
+    ]
+    for copy in copies:
+        copy.start()
+    for copy in copies:
+        copy.wait()
 
 
 def fits(rows, cols, tile_rows, tile_cols, channels, hidden):
@@ -365,13 +429,14 @@
         channels % n == 0
         and channels // n == SUB
         and channels % LANE == 0
-        and rows > 1
+        and rows % 2 == 0
+        and rows > 2
         and cols % 2 == 0
         and hidden == rows * channels
         and pixels == 2 * LANE
         and tile_cols == 2 * SUB
         and radius < min(tile_rows, tile_cols)
-        and (2 * channels) % (cols * 2 * SUB) == 0
+        and channels % (cols * 2 * SUB) == 0
     )
 
 
@@ -389,7 +454,8 @@
     scale = 1.0 / math.sqrt(pixels * n)
     bf16, f32 = jnp.bfloat16, jnp.float32
     flat = (pixels, channels)
-    piece = 2 * channels // cols
+    piece = channels // cols
+    pairs = rows // 2
     vmem = pl.BlockSpec(memory_space=pltpu.VMEM)
     results = pl.pallas_call(
         lambda *refs: fused_kernel(rows, cols, tile_cols, radius, scale, *refs),
@@ -399,14 +465,20 @@
             jax.ShapeDtypeStruct(weight_out.shape, bf16),
             jax.ShapeDtypeStruct(kernel.shape, bf16),
         ),
-        in_specs=[vmem] * 6,
+        in_specs=[pl.BlockSpec(memory_space=pltpu.HBM)] * 6,
         out_specs=(vmem,) * 4,
-        scratch_shapes=[pltpu.VMEM((n, own, pixels), bf16)] * 6 + [
-            pltpu.VMEM((rows, 2 * channels, channels), bf16),
-            pltpu.VMEM((rows, 2 * channels, channels), bf16),
-            pltpu.VMEM((cols, piece, channels), bf16),
-            pltpu.VMEM((cols, piece, channels), bf16),
-            pltpu.VMEM((rows, cols, piece, channels), bf16),
+        scratch_shapes=[pltpu.VMEM(flat, bf16)] * 3 + [
+            pltpu.VMEM(weight_in.shape, bf16),
+            pltpu.VMEM(weight_out.shape, bf16),
+            pltpu.VMEM(kernel.shape, bf16),
+        ] + [pltpu.VMEM((n, own, pixels), bf16)] * 6 + [
+            pltpu.VMEM((2, 2, pairs, channels, channels), bf16),
+            pltpu.VMEM((2, pairs, channels, channels), bf16),
+            pltpu.VMEM((2, pairs, channels, channels), bf16),
+            pltpu.VMEM((2, pairs, channels, channels), bf16),
+            pltpu.VMEM((2, cols, piece, channels), bf16),
+            pltpu.VMEM((2, cols, piece, channels), bf16),
+            pltpu.VMEM((2, 2, pairs, cols, piece, channels), bf16),
             pltpu.VMEM((own, 2 * keep), bf16),
             pltpu.VMEM((n, own, 2 * keep), bf16),
             pltpu.VMEM((n, own, pixels), f32),
@@ -422,16 +494,25 @@
             pltpu.VMEM((pixels, 3 * span), f32),
             pltpu.VMEM((n, 3 * span), bf16),
             pltpu.VMEM((2 * keep, channels), f32),
-            pltpu.SemaphoreType.DMA((8,)),
-            pltpu.SemaphoreType.DMA((8,)),
+            pltpu.SemaphoreType.DMA((6,)),
+            pltpu.SemaphoreType.DMA((16,)),
+            pltpu.SemaphoreType.DMA((16,)),
         ],
         compiler_params=pltpu.CompilerParams(
-            collective_id=0, has_side_effects=True, vmem_limit_bytes=48 * 1024 * 1024
+            collective_id=0, has_side_effects=True, vmem_limit_bytes=64 * 1024 * 1024
         ),
     )(
         inputs.reshape(flat), stored.reshape(flat), upstream.reshape(flat),
         weight_in, weight_out, kernel,
     )
+    results = pl.pallas_call(
+        hand_over_kernel,
+        out_shape=tuple(jax.ShapeDtypeStruct(r.shape, r.dtype) for r in results),
+        in_specs=[pl.BlockSpec(memory_space=pl.ANY)] * len(results),
+        out_specs=(pl.BlockSpec(memory_space=pl.ANY),) * len(results),
+        scratch_shapes=[pltpu.SemaphoreType.DMA((len(results),))],
+        compiler_params=pltpu.CompilerParams(vmem_limit_bytes=64 * 1024 * 1024),
+    )(*results)
     return (results[0].reshape(stored.shape), *results[1:])
 
 

time: 69.1 us -> 103 us (1.49)
  Pallas kernels: 58.5 us -> 102 us
  local copies, waits for them, and re-layouts: 8.8 us -> 0 us
    pallas_call x0 -> x1, Pallas kernels: none -> 50.3 us  [fused_device(): pl.pallas_call(hand_over_kernel, out_shape=tuple((jax.ShapeDtypeStruct(r....]
    unnamed x16 -> x0, local copies, waits for them, and re-layouts: 8.8 us -> none
    pallas_call x1, Pallas kernels: 58.5 us -> 51.9 us  [fused_device(): pl.pallas_call(lambda *refs: fused_kernel(rows, cols, tile_cols, radius,...]
where the time goes in v2:
time: 103 us
  Pallas kernels  102 us (99%)
    pallas_call x1, Pallas kernels, fused_device(): pl.pallas_call(lambda *refs: fused_kernel(rows, cols, tile_cols, radius,...  51.9 us
    pallas_call x1, Pallas kernels, fused_device(): pl.pallas_call(hand_over_kernel, out_shape=tuple((jax.ShapeDtypeStruct(r....  50.3 us

profile of v2, /device:TPU:1, one launch (start us, length us, event | category | flops | bytes accessed | tf_op | source)
XLA Modules:
  0.0 102.8 jit_solution(6674277313195231058)
XLA Ops:
  0.6 51.9 %shard_map.93 = (bf16[256,256]{1,0:T(8,128)(2,1)}, bf16[256,1024]{1,0:T(8,128)(2,1)}, bf16[1024,256]{1,0:T(8,128)(2,1)}, bf16[27,27,256]{2,1,0:T(8,128)(2,1)}) custom-call(bf16[256,256]{1,0:T(8,128)(2,1)} %bitcast.4, bf16[256,256]{1,0:T(8,128)(2,1)} %bitcast.5, bf16[256,256]{1,0:T(8,128)(2,1)} %bitcast.6, bf16[256,1024]{1,0:T(8,128)(2,1)} %refs_3_.1, ...), custom_call_target="tpu_custom_call" | custom-call | tf_op jit(solution)/shard_map/pallas_call | solution.py:460
  52.5 50.3 %shard_map.94 = (bf16[256,256]{1,0:T(8,128)(2,1)}, bf16[256,1024]{1,0:T(8,128)(2,1)}, bf16[1024,256]{1,0:T(8,128)(2,1)}, bf16[27,27,256]{2,1,0:T(8,128)(2,1)}) custom-call(bf16[256,256]{1,0:T(8,128)(2,1)} %get-tuple-element.12.refs_0_, bf16[256,1024]{1,0:T(8,128)(2,1)} %get-tuple-element.13.refs_1_, bf16[1024,256]{1,0:T(8,128)(2,1)} %get-tuple-element.14.refs_2_, ...), custom_call_target="tpu_custom_call" | custom-call | tf_op jit(solution)/shard_map/pallas_call | solution.py:508

commit v3 on v2

--- a/solution.py
+++ b/solution.py
@@ -107,11 +107,13 @@
     return v if shift == 0 else pltpu.roll(v, size - shift, axis)
 
 
-def moved(v, rows, cols, d_row, d_col):
-    tile = lax.broadcasted_iota(jnp.int32, v.shape, 0)
-    row, col = tile // cols + d_row, tile % cols + d_col
-    inside = (row >= 0) & (row < rows) & (col >= 0) & (col < cols)
-    return jnp.where(inside, roll_left(v, d_row * cols + d_col, 0), 0.0)
+def down(v, count):
+    if count == 0:
+        return v
+    blank = jnp.zeros((abs(count), v.shape[1]), v.dtype)
+    if count > 0:
+        return jnp.concatenate([blank, v[:-count]], axis=0)
+    return jnp.concatenate([v[-count:], blank], axis=0)
 
 
 def bytes_of(ref, sem):
@@ -125,7 +127,7 @@
     x_ref, z_ref, g_ref, wi_ref, wo_ref, k_ref,
     x_send, x_recv, g_send, g_recv, o_send, o_recv,
     part, from_pair, paired, from_rows, half, from_cols, allq, gk_send, gk_recv,
-    wide, x3, g3, o3, taps, taps_t, skew, folded, bands, k_mat, m_mat, x_sh, gk_t,
+    wide, x3, g3, o3, taps, taps_t, skew, folded, bands, k_mat, m_mat, x_sh, gk_t, inner,
     isem, ssem, rsem,
 ):
     n = rows * cols
@@ -193,11 +195,14 @@
         mine = allq.at[s, core]
         send(mine, mine, 14 + s, my_row + other - core, my_col)
 
+    row_at = [lax.rem(my_row + r, rows) for r in range(rows)]
+    col_at = [lax.rem(my_col + c, cols) for c in range(cols)]
+
     def to_all(fn):
-        @pl.loop(1, n)
-        def _(p):
-            target = lax.rem(me + p, n)
-            fn(target, target // cols, lax.rem(target, cols))
+        for r in range(rows):
+            for c in range(cols):
+                if r + c:
+                    fn(row_at[r] * cols + col_at[c], row_at[r], col_at[c])
 
     loads = [
         pltpu.make_async_copy(source, target, isem.at[i])
@@ -212,13 +217,7 @@
     to_all(lambda t, r, c: pl.semaphore_signal(
         barrier, inc=1, device_id=(r, c), device_id_type=MESH))
 
-    loads[0].wait()
-    x_send[...] = x_ref[...].astype(f32).T.reshape(n, own, pixels).astype(bf16)
-    x_recv[pl.ds(me, 1)] = x_send[pl.ds(me, 1)]
-    pl.semaphore_wait(barrier, n - 1)
-    to_all(lambda t, r, c: send(x_send.at[t], x_recv.at[me], 0, r, c))
-
-    for load in loads[1:]:
+    for load in loads:
         load.wait()
     z, g = z_ref[...], g_ref[...]
     total = g.astype(f32)
@@ -232,6 +231,11 @@
         total = total + dot(grad_hidden, w_in, 1, 1)
         part[0, f % 2, f // 2] = dot(z, grad_hidden, 0, 0).astype(bf16)
         part[1, f % 2, f // 2] = dot(active, g, 0, 0).astype(bf16)
+        if f == 0:
+            x_send[...] = x_ref[...].astype(f32).T.reshape(n, own, pixels).astype(bf16)
+            x_recv[pl.ds(me, 1)] = x_send[pl.ds(me, 1)]
+            pl.semaphore_wait(barrier, n - 1)
+            to_all(lambda t, r, c: send(x_send.at[t], x_recv.at[me], 0, r, c))
     g_send[...] = total.T.reshape(n, own, pixels).astype(bf16)
     g_recv[pl.ds(me, 1)] = g_send[pl.ds(me, 1)]
     to_all(lambda t, r, c: send(g_send.at[t], g_recv.at[me], 1, r, c))
@@ -256,6 +260,15 @@
         >= lax.broadcasted_iota(jnp.int32, (tile_cols, span), 0)
     )
     offsets = (-1, 0, 1)
+    tile = lax.broadcasted_iota(jnp.int32, (n, pixels), 0) % cols
+    inner[0] = jnp.where(tile > 0, 1.0, 0.0)
+    inner[1] = jnp.where(tile < cols - 1, 1.0, 0.0)
+
+    def aside(v, d_col):
+        if d_col == 0:
+            return v
+        return roll_left(v, d_col, 0) * inner[0 if d_col < 0 else 1]
+
 
     sum_pair(0)
     sum_pair(1)
@@ -271,9 +284,10 @@
     def correlate(c):
         here = x3[c]
         for i, d_col in enumerate(offsets):
+            beside = aside(here, d_col)
             for j, d_row in enumerate(offsets):
                 at = i * span + j * pixels
-                x_sh[:, at:at + pixels] = moved(here, rows, cols, d_row, d_col).astype(bf16)
+                x_sh[:, at:at + pixels] = down(beside, -d_row * cols).astype(bf16)
         m_mat[...] = dot(g3[c].astype(bf16), x_sh[...], 0, 0)
 
         def piece(q, i):
@@ -322,8 +336,10 @@
     keep = gk_send.shape[1] // 2
     lines = (lines * scale)[:, :keep]
     gk_send[...] = jnp.concatenate([lines[:own], lines[own:]], axis=1).astype(bf16)
-    gk_recv[pl.ds(me, 1)] = gk_send[...][None]
-    to_all(lambda t, r, c: send(gk_send, gk_recv.at[me], 2, r, c))
+    spot = gk_recv.at[core, my_pair, my_col]
+    spot[...] = gk_send[...]
+    for p in range(1, cols):
+        send(gk_send, spot, 2, my_row, col_at[p])
 
     sum_cols(0)
     sum_cols(1)
@@ -359,14 +375,20 @@
         spread = dot(here.astype(bf16), k_mat[...], 1, 0)
         result = here
         for i, d_col in enumerate(offsets):
-            for j, d_row in enumerate(offsets):
-                at = i * span + j * pixels
-                result = result + moved(spread[:, at:at + pixels], rows, cols, -d_row, -d_col)
+            at = i * span
+            beside = spread[:, at + pixels:at + 2 * pixels]
+            beside = beside + down(spread[:, at:at + pixels], -cols)
+            beside = beside + down(spread[:, at + 2 * pixels:at + span], cols)
+            result = result + aside(beside, -d_col)
         o3[c] = result
 
     pl.loop(0, own // 2)(convolve)
     share_rows(0)
     share_rows(1)
+    bytes_of(gk_recv.at[0, 0, pl.ds(0, cols - 1)], rsem.at[2])
+    spots = gk_recv.at[core, my_pair]
+    for p in range(1, pairs):
+        send(spots, spots, 16, 2 * lax.rem(my_pair + p, pairs) + core, my_col)
     pl.loop(own // 2, own)(convolve)
 
     for c in range(own):
@@ -377,12 +399,17 @@
 
     share_pair(0)
     share_pair(1)
+    bytes_of(gk_recv.at[0, pl.ds(0, pairs - 1)], rsem.at[16])
+    send(gk_recv.at[core], gk_recv.at[core], 17, my_row + other - core, my_col)
 
     bytes_of(o_recv.at[pl.ds(0, n - 1)], rsem.at[3])
     gi_ref[...] = o_recv[...].astype(f32).reshape(channels, pixels).T.astype(bf16)
 
-    bytes_of(gk_recv.at[pl.ds(0, n - 1)], rsem.at[2])
-    gk_t[...] = gk_recv[...].astype(f32).reshape(channels, 2 * keep).T
+    bytes_of(gk_recv.at[0], rsem.at[17])
+    share = cols * own
+    for r in range(rows):
+        gk_t[:, r * share:(r + 1) * share] = (
+            gk_recv[r % 2, r // 2].astype(f32).reshape(share, 2 * keep).T)
     for a in range(side):
         at = lead + tile_cols * a
         low = gk_t[keep + at + tile_cols - radius:keep + at + tile_cols, :]
@@ -398,7 +425,9 @@
 
     bytes_of(x_send.at[pl.ds(0, n - 1)], ssem.at[0])
     bytes_of(g_send.at[pl.ds(0, n - 1)], ssem.at[1])
-    bytes_of(gk_recv.at[pl.ds(0, n - 1)], ssem.at[2])
+    bytes_of(gk_recv.at[0, 0, pl.ds(0, cols - 1)], ssem.at[2])
+    bytes_of(gk_recv.at[0, pl.ds(0, pairs - 1)], ssem.at[16])
+    bytes_of(gk_recv.at[0], ssem.at[17])
     bytes_of(o_send.at[pl.ds(0, n - 1)], ssem.at[3])
     for s in range(2):
         bytes_of(from_pair.at[s], ssem.at[4 + s])
@@ -409,15 +438,16 @@
         bytes_of(allq.at[s, 0], ssem.at[14 + s])
 
 
-def hand_over_kernel(*refs):
-    count = len(refs) // 2
-    sem = refs[-1]
-    copies = [
-        pltpu.make_async_copy(refs[i], refs[count + i], sem.at[i]) for i in range(count)
-    ]
-    for copy in copies:
+def hand_over_kernel(count, *refs):
+    ins, outs, held, sems = refs[:count], refs[count:2 * count], refs[2 * count:-1], refs[-1]
+    first = [pltpu.make_async_copy(ins[i], held[i], sems.at[0, i]) for i in range(count)]
+    then = [pltpu.make_async_copy(held[i], outs[i], sems.at[1, i]) for i in range(count)]
+    for copy in first:
         copy.start()
-    for copy in copies:
+    for i in range(count):
+        first[i].wait()
+        then[i].start()
+    for copy in then:
         copy.wait()
 
 
@@ -480,7 +510,7 @@
             pltpu.VMEM((2, cols, piece, channels), bf16),
             pltpu.VMEM((2, 2, pairs, cols, piece, channels), bf16),
             pltpu.VMEM((own, 2 * keep), bf16),
-            pltpu.VMEM((n, own, 2 * keep), bf16),
+            pltpu.VMEM((2, pairs, cols, own, 2 * keep), bf16),
             pltpu.VMEM((n, own, pixels), f32),
             pltpu.VMEM((own, n, pixels), f32),
             pltpu.VMEM((own, n, pixels), f32),
@@ -494,9 +524,10 @@
             pltpu.VMEM((pixels, 3 * span), f32),
             pltpu.VMEM((n, 3 * span), bf16),
             pltpu.VMEM((2 * keep, channels), f32),
+            pltpu.VMEM((2, n, pixels), f32),
             pltpu.SemaphoreType.DMA((6,)),
-            pltpu.SemaphoreType.DMA((16,)),
-            pltpu.SemaphoreType.DMA((16,)),
+            pltpu.SemaphoreType.DMA((18,)),
+            pltpu.SemaphoreType.DMA((18,)),
         ],
         compiler_params=pltpu.CompilerParams(
             collective_id=0, has_side_effects=True, vmem_limit_bytes=64 * 1024 * 1024
@@ -506,11 +537,12 @@
         weight_in, weight_out, kernel,
     )
     results = pl.pallas_call(
-        hand_over_kernel,
+        lambda *refs: hand_over_kernel(len(results), *refs),
         out_shape=tuple(jax.ShapeDtypeStruct(r.shape, r.dtype) for r in results),
         in_specs=[pl.BlockSpec(memory_space=pl.ANY)] * len(results),
         out_specs=(pl.BlockSpec(memory_space=pl.ANY),) * len(results),
-        scratch_shapes=[pltpu.SemaphoreType.DMA((len(results),))],
+        scratch_shapes=[pltpu.VMEM(r.shape, r.dtype) for r in results]
+        + [pltpu.SemaphoreType.DMA((2, len(results)))],
         compiler_params=pltpu.CompilerParams(vmem_limit_bytes=64 * 1024 * 1024),
     )(*results)
     return (results[0].reshape(stored.shape), *results[1:])

time: 103 us -> 50.1 us (0.49)
  Pallas kernels: 102 us -> 49.3 us
    pallas_call x1, Pallas kernels: 50.3 us -> 2.29 us  [fused_device(): pl.pallas_call(lambda *refs: hand_over_kernel(len(results), *refs), out_s...]
    pallas_call x1, Pallas kernels: 51.9 us -> 47 us  [fused_device(): pl.pallas_call(lambda *refs: fused_kernel(rows, cols, tile_cols, radius,...]
where the time goes in v3:
time: 50.1 us; the launch traced here: 49.9 us
  Pallas kernels  49.3 us (98%)
  between operations  0.64 us (1%)
    pallas_call x1, Pallas kernels, fused_device(): pl.pallas_call(lambda *refs: fused_kernel(rows, cols, tile_cols, radius,...  47 us
    pallas_call x1, Pallas kernels, fused_device(): pl.pallas_call(lambda *refs: hand_over_kernel(len(results), *refs), out_s...  2.29 us

profile of v3, /device:TPU:1, one launch (start us, length us, event | category | flops | bytes accessed | tf_op | source)
XLA Modules:
  0.0 49.9 jit_solution(15009907887605079863)
XLA Ops:
  0.6 47.0 %shard_map.93 = (bf16[256,256]{1,0:T(8,128)(2,1)}, bf16[256,1024]{1,0:T(8,128)(2,1)}, bf16[1024,256]{1,0:T(8,128)(2,1)}, bf16[27,27,256]{2,1,0:T(8,128)(2,1)}) custom-call(bf16[256,256]{1,0:T(8,128)(2,1)} %bitcast.4, bf16[256,256]{1,0:T(8,128)(2,1)} %bitcast.5, bf16[256,256]{1,0:T(8,128)(2,1)} %bitcast.6, bf16[256,1024]{1,0:T(8,128)(2,1)} %refs_3_.1, ...), custom_call_target="tpu_custom_call" | custom-call | tf_op jit(solution)/shard_map/pallas_call | solution.py:490
  47.6 2.3 %shard_map.94 = (bf16[256,256]{1,0:T(8,128)(2,1)}, bf16[256,1024]{1,0:T(8,128)(2,1)}, bf16[1024,256]{1,0:T(8,128)(2,1)}, bf16[27,27,256]{2,1,0:T(8,128)(2,1)}) custom-call(bf16[256,256]{1,0:T(8,128)(2,1)} %get-tuple-element.12.refs_0_, bf16[256,1024]{1,0:T(8,128)(2,1)} %get-tuple-element.13.refs_1_, bf16[1024,256]{1,0:T(8,128)(2,1)} %get-tuple-element.14.refs_2_, ...), custom_call_target="tpu_custom_call" | custom-call | tf_op jit(solution)/shard_map/pallas_call | solution.py:539

commit v4 on v3

--- a/solution.py
+++ b/solution.py
@@ -126,7 +126,8 @@
     gi_ref, gwi_ref, gwo_ref, gk_ref,
     x_ref, z_ref, g_ref, wi_ref, wo_ref, k_ref,
     x_send, x_recv, g_send, g_recv, o_send, o_recv,
-    part, from_pair, paired, from_rows, half, from_cols, allq, gk_send, gk_recv,
+    part, from_pair, paired, from_rows, half, from_cols, allq,
+    paired_b, from_cols_b, half_b, from_rows_b, all_b, gk_send, gk_recv,
     wide, x3, g3, o3, taps, taps_t, skew, folded, bands, k_mat, m_mat, x_sh, gk_t, inner,
     isem, ssem, rsem,
 ):
@@ -142,6 +143,7 @@
     my_row, my_col = lax.axis_index("row"), lax.axis_index("col")
     me = my_row * cols + my_col
     pairs = rows // 2
+    piece = channels // cols
     my_pair, core = my_row // 2, lax.rem(my_row, 2)
     other = 1 - core
     f32, bf16 = jnp.float32, jnp.bfloat16
@@ -152,48 +154,71 @@
             device_id=(row, col), device_id_type=MESH,
         ).start()
 
-    def sum_pair(s):
-        bytes_of(from_pair.at[s], rsem.at[4 + s])
-        for p in range(pairs):
-            paired[s, p] = (
-                part[s, core, p].astype(f32) + from_pair[s, p].astype(f32)).astype(bf16)
+    def to_pairs(fn):
         for p in range(1, pairs):
             to = lax.rem(my_pair + p, pairs)
-            send(paired.at[s, to], from_rows.at[s, my_pair], 6 + s, 2 * to + core, my_col)
-        from_rows[s, pl.ds(my_pair, 1)] = paired[s, pl.ds(my_pair, 1)]
-
-    def sum_rows(s):
-        bytes_of(from_rows.at[s, pl.ds(0, pairs - 1)], rsem.at[6 + s])
-        v = from_rows[s, 0].astype(f32)
-        for p in range(1, pairs):
-            v = v + from_rows[s, p].astype(f32)
-        half[s] = v.reshape(half.shape[1:]).astype(bf16)
+            fn(to, 2 * to + core, my_col)
+
+    def to_cols(fn):
         for p in range(1, cols):
-            c = lax.rem(my_col + p, cols)
-            send(half.at[s, c], from_cols.at[s, my_col], 8 + s, my_row, c)
-        from_cols[s, pl.ds(my_col, 1)] = half[s, pl.ds(my_col, 1)]
-
-    def sum_cols(s):
-        bytes_of(from_cols.at[s, pl.ds(0, cols - 1)], rsem.at[8 + s])
-        v = from_cols[s, 0].astype(f32)
-        for c in range(1, cols):
-            v = v + from_cols[s, c].astype(f32)
-        mine = allq.at[s, core, my_pair, my_col]
-        mine[...] = (v * scale).astype(bf16)
-        for p in range(1, cols):
-            send(mine, mine, 10 + s, my_row, lax.rem(my_col + p, cols))
-
-    def share_rows(s):
-        bytes_of(allq.at[s, 0, 0, pl.ds(0, cols - 1)], rsem.at[10 + s])
-        mine = allq.at[s, core, my_pair]
-        for p in range(1, pairs):
-            to = lax.rem(my_pair + p, pairs)
-            send(mine, mine, 12 + s, 2 * to + core, my_col)
-
-    def share_pair(s):
-        bytes_of(allq.at[s, 0, pl.ds(0, pairs - 1)], rsem.at[12 + s])
-        mine = allq.at[s, core]
-        send(mine, mine, 14 + s, my_row + other - core, my_col)
+            fn(col_at[p], my_row, col_at[p])
+
+    def added(ref):
+        v = ref[0].astype(f32)
+        for i in range(1, ref.shape[0]):
+            v = v + ref[i].astype(f32)
+        return v
+
+    def sum_pair():
+        bytes_of(from_pair.at[0], rsem.at[4])
+        for p in range(pairs):
+            paired[0, p] = (
+                part[0, core, p].astype(f32) + from_pair[0, p].astype(f32)).astype(bf16)
+        to_pairs(lambda t, r, c: send(paired.at[0, t], from_rows.at[my_pair], 6, r, c))
+        from_rows[pl.ds(my_pair, 1)] = paired[0, pl.ds(my_pair, 1)]
+        bytes_of(from_pair.at[1], rsem.at[5])
+        for p in range(pairs):
+            v = (part[1, core, p].astype(f32) + from_pair[1, p].astype(f32)).astype(bf16)
+            for c in range(cols):
+                paired_b[c, p] = v[c * piece:(c + 1) * piece]
+        to_cols(lambda t, r, c: send(paired_b.at[t], from_cols_b.at[my_col], 7, r, c))
+        from_cols_b[pl.ds(my_col, 1)] = paired_b[pl.ds(my_col, 1)]
+
+    def sum_next():
+        bytes_of(from_rows.at[pl.ds(0, pairs - 1)], rsem.at[6])
+        half[...] = added(from_rows).reshape(half.shape).astype(bf16)
+        to_cols(lambda t, r, c: send(half.at[t], from_cols.at[my_col], 8, r, c))
+        from_cols[pl.ds(my_col, 1)] = half[pl.ds(my_col, 1)]
+        bytes_of(from_cols_b.at[pl.ds(0, cols - 1)], rsem.at[7])
+        half_b[...] = added(from_cols_b).astype(bf16)
+        to_pairs(lambda t, r, c: send(half_b.at[t], from_rows_b.at[my_pair], 9, r, c))
+        from_rows_b[pl.ds(my_pair, 1)] = half_b[pl.ds(my_pair, 1)]
+
+    def sum_last():
+        bytes_of(from_rows_b.at[pl.ds(0, pairs - 1)], rsem.at[9])
+        mine_b = all_b.at[core, my_col, my_pair]
+        mine_b[...] = (added(from_rows_b) * scale).astype(bf16)
+        to_pairs(lambda t, r, c: send(mine_b, mine_b, 11, r, c))
+        bytes_of(from_cols.at[pl.ds(0, cols - 1)], rsem.at[8])
+        mine = allq.at[core, my_pair, my_col]
+        mine[...] = (added(from_cols) * scale).astype(bf16)
+        to_cols(lambda t, r, c: send(mine, mine, 10, r, c))
+
+    def share_first():
+        bytes_of(all_b.at[0, 0, pl.ds(0, pairs - 1)], rsem.at[11])
+        mine_b = all_b.at[core, my_col]
+        to_cols(lambda t, r, c: send(mine_b, mine_b, 13, r, c))
+
+    def share_next():
+        bytes_of(allq.at[0, 0, pl.ds(0, cols - 1)], rsem.at[10])
+        mine = allq.at[core, my_pair]
+        to_pairs(lambda t, r, c: send(mine, mine, 12, r, c))
+
+    def share_pair():
+        bytes_of(all_b.at[0, pl.ds(0, cols - 1)], rsem.at[13])
+        send(all_b.at[core], all_b.at[core], 15, my_row + other - core, my_col)
+        bytes_of(allq.at[0, pl.ds(0, pairs - 1)], rsem.at[12])
+        send(allq.at[core], allq.at[core], 14, my_row + other - core, my_col)
 
     row_at = [lax.rem(my_row + r, rows) for r in range(rows)]
     col_at = [lax.rem(my_col + c, cols) for c in range(cols)]
@@ -260,6 +285,12 @@
         >= lax.broadcasted_iota(jnp.int32, (tile_cols, span), 0)
     )
     offsets = (-1, 0, 1)
+
+    def window(q_first, q_last):
+        low = (lead + q_first * tile_cols) // LANE * LANE
+        high = round_up(lead + (q_last + 1) * tile_cols - 1 + side * tile_cols, LANE)
+        return low, min(high, span)
+
     tile = lax.broadcasted_iota(jnp.int32, (n, pixels), 0) % cols
     inner[0] = jnp.where(tile > 0, 1.0, 0.0)
     inner[1] = jnp.where(tile < cols - 1, 1.0, 0.0)
@@ -270,8 +301,7 @@
         return roll_left(v, d_col, 0) * inner[0 if d_col < 0 else 1]
 
 
-    sum_pair(0)
-    sum_pair(1)
+    sum_pair()
     bytes_of(x_recv.at[pl.ds(0, n - 1)], rsem.at[0])
     wide[...] = x_recv[...].astype(f32)
     for c in range(own):
@@ -290,31 +320,37 @@
                 x_sh[:, at:at + pixels] = down(beside, -d_row * cols).astype(bf16)
         m_mat[...] = dot(g3[c].astype(bf16), x_sh[...], 0, 0)
 
-        def piece(q, i):
-            return m_mat[q * tile_cols:(q + 1) * tile_cols, i * span:(i + 1) * span]
-
-        def lagged(q, sign):
+        def lagged(q, sign, low, high):
             after, before = ((1, 2), (0, 1))[sign]
-            out = jnp.zeros((tile_cols, span), f32)
+            mask = at_or_after[:, :high - low]
+
+            def block_of(q, i):
+                return m_mat[
+                    q * tile_cols:(q + 1) * tile_cols, i * span + low:i * span + high]
+
+            out = None
             if q >= 1:
-                out = jnp.where(at_or_after, piece(q - 1, after), 0.0)
+                out = jnp.where(mask, block_of(q - 1, after), 0.0)
             if q < chunks:
-                out = out + jnp.where(at_or_after, 0.0, piece(q, before))
+                more = jnp.where(mask, 0.0, block_of(q, before))
+                out = more if out is None else out + more
             return out
 
         for sign in range(2):
             parts = []
             for i in range(per_block):
-                v = jnp.zeros((tile_cols, width), f32)
+                columns = [None] * (width // LANE)
                 for q in range(i, chunks + 1, per_block):
-                    skip = q // per_block * LANE
-                    piece_q = lagged(q, sign)[:, skip:skip + width]
-                    missing = width - piece_q.shape[1]
-                    if missing:
-                        piece_q = jnp.concatenate(
-                            [piece_q, jnp.zeros((tile_cols, missing), f32)], axis=1)
-                    v = v + piece_q
-                parts.append(v)
+                    low, high = window(q, q)
+                    v = lagged(q, sign, low, high)
+                    first = low // LANE - q // per_block
+                    for k in range((high - low) // LANE):
+                        u = v[:, k * LANE:(k + 1) * LANE]
+                        old = columns[first + k]
+                        columns[first + k] = u if old is None else old + u
+                blank = jnp.zeros((tile_cols, LANE), f32)
+                parts.append(jnp.concatenate(
+                    [blank if u is None else u for u in columns], axis=1))
             while len(parts) > 1:
                 m = len(parts) // 2
                 parts = [parts[i] + roll_left(parts[i + m], m * tile_cols, 1) for i in range(m)]
@@ -326,8 +362,7 @@
             folded[sign * own + c] = v
 
     pl.loop(0, own // 2)(correlate)
-    sum_rows(0)
-    sum_rows(1)
+    sum_next()
     pl.loop(own // 2, own)(correlate)
 
     lines = folded[:, 0, :]
@@ -341,8 +376,7 @@
     for p in range(1, cols):
         send(gk_send, spot, 2, my_row, col_at[p])
 
-    sum_cols(0)
-    sum_cols(1)
+    sum_last()
 
     bands[...] = jnp.zeros_like(bands)
 
@@ -360,17 +394,20 @@
             for i, u in enumerate(parts):
                 bands[sign, i * tile_cols:(i + 1) * tile_cols, pixels:pixels + width] = u
 
-        def band(q, sign):
+        def band(q, sign, low, high):
             at = q % per_block * tile_cols
             skip = pixels - q // per_block * LANE
-            return bands[sign, at:at + tile_cols, skip:skip + span]
+            return bands[sign, at:at + tile_cols, skip + low:skip + high]
 
         for q in range(chunks):
             at = slice(q * tile_cols, (q + 1) * tile_cols)
-            k_mat[at, :span] = jnp.where(at_or_after, band(q + 1, 1), 0.0).astype(bf16)
-            k_mat[at, span:2 * span] = jnp.where(
-                at_or_after, band(q + 1, 0), band(q, 1)).astype(bf16)
-            k_mat[at, 2 * span:] = jnp.where(at_or_after, 0.0, band(q, 0)).astype(bf16)
+            low, high = window(q, q + 1)
+            mask = at_or_after[:, :high - low]
+            k_mat[at, low:high] = jnp.where(mask, band(q + 1, 1, low, high), 0.0).astype(bf16)
+            k_mat[at, span + low:span + high] = jnp.where(
+                mask, band(q + 1, 0, low, high), band(q, 1, low, high)).astype(bf16)
+            k_mat[at, 2 * span + low:2 * span + high] = jnp.where(
+                mask, 0.0, band(q, 0, low, high)).astype(bf16)
         here = g3[c]
         spread = dot(here.astype(bf16), k_mat[...], 1, 0)
         result = here
@@ -382,9 +419,11 @@
             result = result + aside(beside, -d_col)
         o3[c] = result
 
-    pl.loop(0, own // 2)(convolve)
-    share_rows(0)
-    share_rows(1)
+    k_mat[...] = jnp.zeros_like(k_mat)
+    pl.loop(0, own // 4)(convolve)
+    share_first()
+    pl.loop(own // 4, own // 2)(convolve)
+    share_next()
     bytes_of(gk_recv.at[0, 0, pl.ds(0, cols - 1)], rsem.at[2])
     spots = gk_recv.at[core, my_pair]
     for p in range(1, pairs):
@@ -397,8 +436,7 @@
     o_recv[pl.ds(me, 1)] = o_send[pl.ds(me, 1)]
     to_all(lambda t, r, c: send(o_send.at[t], o_recv.at[me], 3, r, c))
 
-    share_pair(0)
-    share_pair(1)
+    share_pair()
     bytes_of(gk_recv.at[0, pl.ds(0, pairs - 1)], rsem.at[16])
     send(gk_recv.at[core], gk_recv.at[core], 17, my_row + other - core, my_col)
 
@@ -416,12 +454,13 @@
         high = gk_t[at:at + radius + 1, :]
         gk_ref[a] = jnp.concatenate([low, high], axis=0).astype(bf16)
 
-    for s in range(2):
-        bytes_of(allq.at[s, 0], rsem.at[14 + s])
+    bytes_of(all_b.at[0], rsem.at[15])
+    bytes_of(allq.at[0], rsem.at[14])
     for f in range(rows):
         at = slice(f * block, (f + 1) * block)
-        gwi_ref[:, at] = allq[0, f % 2, f // 2].reshape(channels, block)
-        gwo_ref[at, :] = allq[1, f % 2, f // 2].reshape(block, channels)
+        gwi_ref[:, at] = allq[f % 2, f // 2].reshape(channels, block)
+        for c in range(cols):
+            gwo_ref[f * block + c * piece:f * block + (c + 1) * piece, :] = all_b[f % 2, c, f // 2]
 
     bytes_of(x_send.at[pl.ds(0, n - 1)], ssem.at[0])
     bytes_of(g_send.at[pl.ds(0, n - 1)], ssem.at[1])
@@ -431,11 +470,16 @@
     bytes_of(o_send.at[pl.ds(0, n - 1)], ssem.at[3])
     for s in range(2):
         bytes_of(from_pair.at[s], ssem.at[4 + s])
-        bytes_of(paired.at[s, pl.ds(0, pairs - 1)], ssem.at[6 + s])
-        bytes_of(half.at[s, pl.ds(0, cols - 1)], ssem.at[8 + s])
-        bytes_of(from_cols.at[s, pl.ds(0, cols - 1)], ssem.at[10 + s])
-        bytes_of(allq.at[s, 0, pl.ds(0, pairs - 1)], ssem.at[12 + s])
-        bytes_of(allq.at[s, 0], ssem.at[14 + s])
+    bytes_of(paired.at[0, pl.ds(0, pairs - 1)], ssem.at[6])
+    bytes_of(paired_b.at[pl.ds(0, cols - 1)], ssem.at[7])
+    bytes_of(half.at[pl.ds(0, cols - 1)], ssem.at[8])
+    bytes_of(half_b.at[pl.ds(0, pairs - 1)], ssem.at[9])
+    bytes_of(half.at[pl.ds(0, cols - 1)], ssem.at[10])
+    bytes_of(half_b.at[pl.ds(0, pairs - 1)], ssem.at[11])
+    bytes_of(allq.at[0, pl.ds(0, pairs - 1)], ssem.at[12])
+    bytes_of(all_b.at[0, pl.ds(0, cols - 1)], ssem.at[13])
+    bytes_of(allq.at[0], ssem.at[14])
+    bytes_of(all_b.at[0], ssem.at[15])
 
 
 def hand_over_kernel(count, *refs):
@@ -504,11 +548,16 @@
         ] + [pltpu.VMEM((n, own, pixels), bf16)] * 6 + [
             pltpu.VMEM((2, 2, pairs, channels, channels), bf16),
             pltpu.VMEM((2, pairs, channels, channels), bf16),
-            pltpu.VMEM((2, pairs, channels, channels), bf16),
-            pltpu.VMEM((2, pairs, channels, channels), bf16),
-            pltpu.VMEM((2, cols, piece, channels), bf16),
-            pltpu.VMEM((2, cols, piece, channels), bf16),
-            pltpu.VMEM((2, 2, pairs, cols, piece, channels), bf16),
+            pltpu.VMEM((1, pairs, channels, channels), bf16),
+            pltpu.VMEM((pairs, channels, channels), bf16),
+            pltpu.VMEM((cols, piece, channels), bf16),
+            pltpu.VMEM((cols, piece, channels), bf16),
+            pltpu.VMEM((2, pairs, cols, piece, channels), bf16),
+            pltpu.VMEM((cols, pairs, piece, channels), bf16),
+            pltpu.VMEM((cols, pairs, piece, channels), bf16),
+            pltpu.VMEM((pairs, piece, channels), bf16),
+            pltpu.VMEM((pairs, piece, channels), bf16),
+            pltpu.VMEM((2, cols, pairs, piece, channels), bf16),
             pltpu.VMEM((own, 2 * keep), bf16),
             pltpu.VMEM((2, pairs, cols, own, 2 * keep), bf16),
             pltpu.VMEM((n, own, pixels), f32),

time: 50.1 us -> 46.1 us (0.920)
  Pallas kernels: 49.3 us -> 44.9 us
    pallas_call x1, Pallas kernels: 47 us -> 42.6 us  [fused_device(): pl.pallas_call(lambda *refs: fused_kernel(rows, cols, tile_cols, radius,...]
where the time goes in v4:
time: 46.1 us; the launch traced here: 45.6 us
  Pallas kernels  44.9 us (97%)
  between operations  0.64 us (1%)
    pallas_call x1, Pallas kernels, fused_device(): pl.pallas_call(lambda *refs: fused_kernel(rows, cols, tile_cols, radius,...  42.6 us
    pallas_call x1, Pallas kernels, fused_device(): pl.pallas_call(lambda *refs: hand_over_kernel(len(results), *refs), out_s...  2.29 us

profile of v4, /device:TPU:1, one launch (start us, length us, event | category | flops | bytes accessed | tf_op | source)
XLA Modules:
  0.0 45.6 jit_solution(11599555184797320260)
XLA Ops:
  0.6 42.6 %shard_map.93 = (bf16[256,256]{1,0:T(8,128)(2,1)}, bf16[256,1024]{1,0:T(8,128)(2,1)}, bf16[1024,256]{1,0:T(8,128)(2,1)}, bf16[27,27,256]{2,1,0:T(8,128)(2,1)}) custom-call(bf16[256,256]{1,0:T(8,128)(2,1)} %bitcast.4, bf16[256,256]{1,0:T(8,128)(2,1)} %bitcast.5, bf16[256,256]{1,0:T(8,128)(2,1)} %bitcast.6, bf16[256,1024]{1,0:T(8,128)(2,1)} %refs_3_.1, ...), custom_call_target="tpu_custom_call" | custom-call | tf_op jit(solution)/shard_map/pallas_call | solution.py:534
  43.3 2.3 %shard_map.94 = (bf16[256,256]{1,0:T(8,128)(2,1)}, bf16[256,1024]{1,0:T(8,128)(2,1)}, bf16[1024,256]{1,0:T(8,128)(2,1)}, bf16[27,27,256]{2,1,0:T(8,128)(2,1)}) custom-call(bf16[256,256]{1,0:T(8,128)(2,1)} %get-tuple-element.12.refs_0_, bf16[256,1024]{1,0:T(8,128)(2,1)} %get-tuple-element.13.refs_1_, bf16[1024,256]{1,0:T(8,128)(2,1)} %get-tuple-element.14.refs_2_, ...), custom_call_target="tpu_custom_call" | custom-call | tf_op jit(solution)/shard_map/pallas_call | solution.py:588
